TPU v7x, 256 devices: a whole 4x4x8 slice. The times are simulated.
256 devices in a mesh: group: 16 (over z, x_hi), tp: 16 (over x_lo, y, core).
Axes of the slice: x: 4 (x_hi: 2, x_lo: 2; x = x_hi * 2 + x_lo), y: 4, z: 8, core: 2. Of those that a mesh axis runs over, the one named last changes fastest.
Arguments:
- hidden_in: bfloat16 [16, 8, 4, 5120], P('group'), may hold values from -6 to 6
- q_weight: bfloat16 [5120, 4096], P(None, 'tp'), may hold values from -0.078125 to 0.078125
- kv_weight: bfloat16 [5120, 1024], P(None, 'tp'), may hold values from -0.078125 to 0.078125
- o_weight: bfloat16 [4096, 5120], P('tp'), may hold values from -0.09375 to 0.09375
- q_gain: float32 [128], replicated, may hold values from 1 to 8
- k_gain: float32 [128], replicated, may hold values from 1 to 8
- cache: bfloat16 [16, 8, 2, 4, 4096, 128], P('group', None, None, None, 'tp'), may hold values from -6 to 6
- lengths: int32 [16, 8], P('group'), may hold values from 1 to 4092, 16384 in all within a row
- owner: int32 [16], replicated, may hold values from 0 to 15, each once
- a_q: bfloat16 [5120, 64], P('group'), may hold values from -0.078125 to 0.078125
- b_q: bfloat16 [64, 4096], P('group', 'tp'), may hold values from -0.75 to 0.75
- a_o: bfloat16 [4096, 64], P('tp', 'group'), may hold values from -0.09375 to 0.09375
- b_o: bfloat16 [64, 5120], P('group', 'tp'), may hold values from -0.75 to 0.75
Outputs:
- attn_out: bfloat16 [16, 8, 4, 5120], P('group', None, None, 'tp')
Inputs may be any that keep to these rules, and one draw needn't show every extreme that they name: In each group the sequences' lengths sum to 16384 and the largest is 4092. `owner`: a permutation of the group indices.
All inputs are finite; a program needn't handle non-finite values.
Results may differ from a plain program's by a relative error of at most 0.012.
Values may be sent and summed in bfloat16 or wider, within the bound.
No kernel may reach another device: no remote copies, remote signals or barrier semaphores. Data moves between devices by JAX's collectives and lax.ppermute only.
A program may use at most 64 MiB of HBM per device.

v0:
```python
import math

import jax
import jax.numpy as jnp
from jax import lax
from jax.sharding import PartitionSpec as P

HD = 128
QH = 32
KVH = 4
R = 64


def joined(value, axis, combine):
    everything = jax.tree.map(lambda part: lax.all_gather(part, axis), value)
    initial = jax.tree.map(lambda part: part[0], everything)

    def turn(k, so_far):
        return combine(so_far, jax.tree.map(lambda part: part[k], everything))

    return lax.fori_loop(1, lax.axis_size(axis), turn, initial)


def scaled_norm(values, gain_vec):
    mean_square = jnp.mean(values * values, axis=-1, keepdims=True)
    return values * lax.rsqrt(mean_square + 1e-06) * gain_vec


def join_parts(earlier_part, later_part):
    largest = jnp.maximum(earlier_part[0], later_part[0])
    left_scale = jnp.exp(earlier_part[0] - largest)
    right_scale = jnp.exp(later_part[0] - largest)
    sum_total = earlier_part[1] * left_scale + later_part[1] * right_scale
    weighted = earlier_part[2] * left_scale[..., None] + later_part[2] * right_scale[..., None]
    return (largest, sum_total, weighted)


def per_device(
    hidden_in,
    q_weight,
    kv_weight,
    o_weight,
    q_gain,
    k_gain,
    cache,
    lengths,
    owner,
    a_q,
    b_q,
    a_o,
    b_o,
):
    seq_count = hidden_in.shape[1]
    step_count = hidden_in.shape[2]
    model_width = hidden_in.shape[3]
    row_count = seq_count * step_count
    tokens = hidden_in.reshape(row_count, model_width)
    groups = lax.axis_size("group")
    factor_a, gathered_bq, gathered_ao, gathered_bo = (
        lax.all_gather(a_q, "group", axis=0, tiled=True),
        lax.all_gather(b_q, "group", axis=0, tiled=True),
        lax.all_gather(a_o, "group", axis=1, tiled=True),
        lax.all_gather(b_o, "group", axis=0, tiled=True),
    )
    block_rows = factor_a.shape[0] // groups
    owner_match = (owner[None, :] == jnp.arange(groups, dtype=jnp.int32)[:, None]).astype(
        jnp.bfloat16
    )
    a_true = jnp.einsum(
        "bj,jkr->bkr",
        owner_match,
        factor_a.reshape(groups, block_rows, R),
        preferred_element_type=jnp.float32,
    )
    a_true = a_true.astype(jnp.bfloat16).reshape(model_width, R)
    low_query = jnp.dot(tokens, a_true, preferred_element_type=jnp.float32)
    query_part = jnp.dot(tokens, q_weight, preferred_element_type=jnp.float32) + 0.5 * jnp.dot(
        low_query, gathered_bq.astype(jnp.float32), precision=lax.Precision.HIGHEST
    )
    keyval_part = jnp.dot(tokens, kv_weight, preferred_element_type=jnp.float32)
    query_full, keyval_full = (
        lax.all_gather(query_part, "tp", axis=1, tiled=True),
        lax.all_gather(keyval_part, "tp", axis=1, tiled=True),
    )
    key_width = KVH * HD
    queries = scaled_norm(query_full.reshape(seq_count, step_count, QH, HD), q_gain).astype(
        jnp.bfloat16
    )
    new_keys = scaled_norm(
        keyval_full[:, :key_width].reshape(seq_count, step_count, KVH, HD), k_gain
    ).astype(jnp.bfloat16)
    new_values = (
        keyval_full[:, key_width:].reshape(seq_count, step_count, KVH, HD).astype(jnp.bfloat16)
    )
    grouped = queries.reshape(seq_count, step_count, KVH, QH // KVH, HD)
    inv_root = 1.0 / math.sqrt(HD)
    slot_count = cache.shape[4]
    first_slot = lax.axis_index("tp") * slot_count
    position = first_slot + jnp.arange(slot_count, dtype=jnp.int32)
    is_valid = (position[None, :] < lengths[0][:, None])[:, None, None, None, :]
    scores = (
        jnp.einsum("stcgh,scph->stcgp", grouped, cache[0, :, 0], preferred_element_type=jnp.float32)
        * inv_root
    )
    scores = jnp.where(is_valid, scores, -1e30)
    local_max = scores.max(-1)
    weights = jnp.where(is_valid, jnp.exp(scores - local_max[..., None]), 0.0)
    local_total = weights.sum(-1)
    local_out = jnp.einsum(
        "stcgp,scph->stcgh",
        weights.astype(jnp.bfloat16),
        cache[0, :, 1],
        preferred_element_type=jnp.float32,
    )
    local_max = local_max.reshape(seq_count, step_count, QH)
    local_total = local_total.reshape(seq_count, step_count, QH)
    local_out = local_out.reshape(seq_count, step_count, QH, HD)
    own_heads = QH // lax.axis_size("tp")
    offset = lax.axis_index("tp") * own_heads
    merged_parts = joined((local_max, local_total, local_out), "tp", join_parts)
    cache_part = tuple(
        (lax.dynamic_slice_in_dim(member, offset, own_heads, 2) for member in merged_parts)
    )
    fresh_scores = (
        jnp.einsum("stcgh,such->stcgu", grouped, new_keys, preferred_element_type=jnp.float32)
        * inv_root
    )
    causal = (jnp.arange(step_count)[:, None] >= jnp.arange(step_count)[None, :])[
        None, :, None, None, :
    ]
    fresh_scores = jnp.where(causal, fresh_scores, -1e30)
    fresh_max = fresh_scores.max(-1)
    fresh_weights = jnp.where(causal, jnp.exp(fresh_scores - fresh_max[..., None]), 0.0)
    fresh_total = fresh_weights.sum(-1)
    fresh_out = jnp.einsum(
        "stcgu,such->stcgh",
        fresh_weights.astype(jnp.bfloat16),
        new_values,
        preferred_element_type=jnp.float32,
    )
    fresh_part = (
        lax.dynamic_slice_in_dim(
            fresh_max.reshape(seq_count, step_count, QH), offset, own_heads, 2
        ),
        lax.dynamic_slice_in_dim(
            fresh_total.reshape(seq_count, step_count, QH), offset, own_heads, 2
        ),
        lax.dynamic_slice_in_dim(
            fresh_out.reshape(seq_count, step_count, QH, HD), offset, own_heads, 2
        ),
    )
    combined = join_parts(cache_part, fresh_part)
    attended = (
        (combined[2] / combined[1][..., None])
        .reshape(row_count, own_heads * HD)
        .astype(jnp.bfloat16)
    )
    partial_value = jnp.dot(attended, o_weight, preferred_element_type=jnp.float32)
    low_part = jnp.dot(attended, gathered_ao, preferred_element_type=jnp.float32)
    low_sum = lax.psum(low_part, "tp")
    extra_term = 0.5 * jnp.dot(
        low_sum, gathered_bo.astype(jnp.float32), precision=lax.Precision.HIGHEST
    )
    result = lax.psum_scatter(partial_value, "tp", scatter_dimension=1, tiled=True) + extra_term
    return result.astype(jnp.bfloat16).reshape(1, seq_count, step_count, result.shape[1])


def solution(mesh):
    placed = (
        P("group", None, None, None),
        P(None, "tp"),
        P(None, "tp"),
        P("tp", None),
        P(),
        P(),
        P("group", None, None, None, "tp", None),
        P("group", None),
        P(),
        P("group", None),
        P("group", "tp"),
        P("tp", "group"),
        P("group", "tp"),
    )
    return jax.shard_map(
        per_device,
        mesh=mesh,
        in_specs=placed,
        out_specs=P("group", None, None, "tp"),
        check_vma=False,
    )
```

profile of v0, /device:TPU:1, one launch (start us, length us, event | category | flops | bytes accessed | tf_op | source)
XLA Modules:
  0.0 374.3 jit_solution(3406429298113805049)
XLA Ops:
  6.5 38.0 %all-gather.1 = bf16[16,4,256]{2,1,0:T(4,128)(2,1)S(1)} all-gather(bf16[1,4,256]{2,1,0:T(4,128)(2,1)} %bitcast.145), channel_id=1, replica_groups=mesh['group'=16,'tp'=16] {'group'}, dimensions={0}, use_global_device_ids=true | all-gather | bytes 34816 | tf_op jit(solution)/shard_map/all_gather | solution.py:61
  45.6 34.6 %all-gather = bf16[16,320,64]{1,2,0:T(8,128)(2,1)S(1)} all-gather(bf16[1,320,64]{1,2,0:T(8,128)(2,1)} %bitcast.143), channel_id=1, replica_groups=mesh['group'=16,'tp'=16] {'group'}, dimensions={0}, use_global_device_ids=true | all-gather | bytes 696320 | tf_op jit(solution)/shard_map/all_gather | solution.py:60
  80.1 2.1 convolution_convert_fusion
  82.2 2.4 reshape.112
  84.7 2.4 fusion.67
  87.5 34.3 %all_gather.29 = f32[32,4096]{1,0:T(8,128)S(1)} all-gather(f32[32,256]{1,0:T(8,128)S(1)} %fusion.26), channel_id=1, replica_groups=mesh['group'=16,'tp'=16] {'tp'}, dimensions={1}, use_global_device_ids=true | all-gather | bytes 557056 | tf_op jit(solution)/shard_map/all_gather | solution.py:82
  123.3 2.7 fusion.66
  127.0 2.1 fusion.19
  131.5 17.6 %all-gather.2 = f32[16,64,32]{1,2,0:T(8,128)S(1)} all-gather(f32[1,64,32]{1,2,0:T(8,128)S(1)} %convolution_bitcast_fusion.2), channel_id=1, replica_groups=mesh['group'=16,'tp'=16] {'tp'}, dimensions={0}, use_global_device_ids=true | all-gather | bytes 139264 | tf_op jit(solution)/shard_map/all_gather | solution.py:83
  153.3 2.2 fusion.65
  159.3 1.6 fusion.28
  161.1 19.6 %all_gather.31 = f32[16,8,4,32]{3,1,2,0:T(8,128)S(1)} all-gather(f32[1,8,4,32]{3,1,2,0:T(8,128)S(1)} %all_gather_reshape.10), channel_id=1, replica_groups=mesh['group'=16,'tp'=16] {'tp'}, dimensions={0}, use_global_device_ids=true | all-gather | bytes 69632 | tf_op jit(solution)/shard_map/all_gather | solution.py:15
  180.7 17.0 %all_gather.30 = f32[16,8,4,32]{3,1,2,0:T(8,128)S(1)} all-gather(f32[1,8,4,32]{3,1,2,0:T(8,128)S(1)} %all_gather_reshape.9), channel_id=1, replica_groups=mesh['group'=16,'tp'=16] {'tp'}, dimensions={0}, use_global_device_ids=true | all-gather | bytes 69632 | tf_op jit(solution)/shard_map/all_gather | solution.py:15
  199.6 34.9 %while.19 = (s32[]{:T(128)}, f32[8,4,32]{2,1,0:T(4,128)S(1)}, f32[8,4,32]{2,1,0:T(4,128)S(1)}, f32[8,4,32,128]{3,2,1,0:T(8,128)S(1)}, f32[16,8,4,32]{3,1,2,0:T(8...) while((s32[]{:T(128)}, f32[8,4,32]{2,1,0:T(4,128)S(1)}, ...), condition=%wide.region_4.5_spmd, body=%wide.region_3.4_spmd.sunk | while | flops 399365 | bytes 1630351 | solution.py:21
  200.3 1.5 fusion.84
  202.7 1.5 fusion.84
  205.0 1.5 fusion.84
  207.3 1.5 fusion.84
  209.6 1.5 fusion.84
  212.0 1.5 fusion.84
  214.3 1.5 fusion.84
  216.6 1.5 fusion.84
  218.9 1.5 fusion.84
  221.3 1.5 fusion.84
  223.6 1.5 fusion.84
  225.9 1.5 fusion.84
  230.6 1.5 fusion.84
  232.9 1.5 fusion.84
  236.7 2.7 convolution_bitcast_fusion
  240.1 33.6 %all-gather.3 = bf16[16,4,256]{2,1,0:T(4,128)(2,1)S(1)} all-gather(bf16[1,4,256]{2,1,0:T(4,128)(2,1)S(1)} %bitcast.146), channel_id=1, replica_groups=mesh['group'=16,'tp'=16] {'group'}, dimensions={0}, use_global_device_ids=true | all-gather | bytes 34816 | tf_op jit(solution)/shard_map/all_gather | solution.py:62
  273.8 29.0 %all-gather.4 = bf16[16,4,320]{2,1,0:T(4,128)(2,1)S(1)} all-gather(bf16[1,4,320]{2,1,0:T(4,128)(2,1)S(1)} %bitcast.144), channel_id=1, replica_groups=mesh['group'=16,'tp'=16] {'group'}, dimensions={0}, use_global_device_ids=true | all-gather | bytes 43520 | tf_op jit(solution)/shard_map/all_gather | solution.py:63
  302.9 62.8 %psum.7 = f32[32,64]{1,0:T(8,128)S(1)} all-reduce(f32[32,64]{1,0:T(8,128)S(1)} %fusion.46), channel_id=1, replica_groups=mesh['group'=16,'tp'=16] {'tp'}, use_global_device_ids=true, to_apply=%region_9.10 | all-reduce | flops 2048 | bytes 16384 | tf_op jit(solution)/shard_map/psum | solution.py:160
  (113 shorter events, 34.1 us)
Async XLA Ops:
  6.5 230.2 %copy-start = (bf16[256,5120]{1,0:T(8,128)(2,1)S(1)}, bf16[256,5120]{1,0:T(8,128)(2,1)}, u32[]{:S(2)}) copy-start(bf16[256,5120]{1,0:T(8,128)(2,1)} %param.18) | copy-start | bytes 7864324
  6.5 191.9 %all-gather.7.cloned.1.call-start = ((), (), s32[]{:S(2)}) async-start(), calls=%async_computation.1 | async-start | bytes 8912896 | tf_op jit(solution)/shard_map/all_gather | solution.py:15
  84.7 2.4 copy-start.1
  87.0 36.2 %copy-start.10 = (s32[1,8]{1,0:T(1,128)S(1)}, s32[1,8]{1,0:T(1,128)}, u32[]{:S(2)}) copy-start(s32[1,8]{1,0:T(1,128)} %param.22) | copy-start | bytes 100
  87.1 36.2 %copy-start.11 = (f32[128]{0:T(128)S(1)}, f32[128]{0:T(128)}, u32[]{:S(2)}) copy-start(f32[128]{0:T(128)} %param.19) | copy-start | bytes 1540
  123.2 2.8 copy-start.6
  126.0 1.0 copy-start.2
  129.1 24.1 %copy-start.9 = (f32[128]{0:T(128)S(1)}, f32[128]{0:T(128)}, u32[]{:S(2)}) copy-start(f32[128]{0:T(128)} %param.20) | copy-start | bytes 1540
  129.1 24.2 %copy-start.3 = (f32[4,8,32,128]{3,2,1,0:T(8,128)S(1)}, f32[4,8,32,128]{3,2,1,0:T(8,128)}, u32[]{:S(2)}) copy-start(f32[4,8,32,128]{3,2,1,0:T(8,128)} %copy.145) | copy-start | bytes 1572868
  130.1 235.6 %reduce-scatter.4.cloned.1.call-start = ((), (), s32[]{:S(2)}) async-start(), calls=%async_computation.2 | async-start | bytes 2785280
  155.5 3.7 copy-start.5
  197.7 0.7 copy-start.4
  239.4 0.7 copy-start.8
  239.4 34.3 %copy-start.7 = (bf16[4,320]{1,0:T(4,128)(2,1)S(1)}, bf16[4,320]{1,0:T(4,128)(2,1)}, u32[]{:S(2)}) copy-start(bf16[4,320]{1,0:T(4,128)(2,1)} %param.27) | copy-start | bytes 7684
Sparse Core Ops, SparseCore 0:
  130.2 52.1 all-gather.6
  239.6 60.3 reduce-scatter.3
where the time goes:
time: 380 us; the launch traced here: 374 us
  blocking collectives  286 us (75%)
  local copies, waits for them, and re-layouts  28.5 us (8%)
  other arithmetic  27.9 us (7%)
  matrix products  17.4 us (5%)
  between operations  13.7 us (4%)
    psum x1, blocking collectives, per_device(): low_sum = lax.psum(low_part, 'tp')  62.8 us
    all_gather x1, blocking collectives, per_device(): lax.all_gather(b_q, 'group', axis=0, tiled=True)  38 us
    all_gather x2, blocking collectives, joined(): everything = jax.tree.map(lambda part: lax.all_gather(part, axis), value)  36.6 us
    all_gather x1, blocking collectives, per_device(): lax.all_gather(a_q, 'group', axis=0, tiled=True)  34.6 us
    all_gather x1, blocking collectives, per_device(): lax.all_gather(query_part, 'tp', axis=1, tiled=True)  34.3 us
    all_gather x1, blocking collectives, per_device(): lax.all_gather(a_o, 'group', axis=1, tiled=True)  33.6 us
    all_gather x1, blocking collectives, per_device(): lax.all_gather(b_o, 'group', axis=0, tiled=True)  29 us
    add x15, other arithmetic, join_parts(): earlier_part[2] * left_scale[..., None]  23.1 us
  transfers between devices with their start and end apart: 2, of which 0 were waited for; matrix products, arithmetic and copies ran while one was open for 4% of the time, Pallas kernels for 0%

commit v1 on v0

v1 whole, which is shorter than its diff:
```python
import functools
import math

import jax
import jax.numpy as jnp
from jax import lax
from jax.experimental import pallas as pl
from jax.experimental.pallas import tpu as pltpu
from jax.sharding import PartitionSpec as P

HD = 128
QH = 32
KVH = 4
R = 64
TP = 16
GROUPS = 16
SEQS = 8
STEPS = 4
ROWS = SEQS * STEPS
PER_SEQ = 2 * STEPS
WIDTH = 5120
SLOTS = 256
BLOCK = WIDTH // GROUPS
HALF = BLOCK // 2
OUT = WIDTH // TP
INV_ROOT = 1.0 / math.sqrt(HD)
FAR = -1e30
BF16 = jnp.bfloat16
F32 = jnp.float32

BQ_AT = 80
AO_AT = 88
BO_AT = 96
FACTOR_ROWS = 112
QKV_ROWS = 96
PART_ROWS = 80

VMEM = pl.BlockSpec(memory_space=pltpu.VMEM)
SMEM = pl.BlockSpec(memory_space=pltpu.SMEM)
NT = (((1,), (1,)), ((), ()))


def lanes(shape):
    return lax.broadcasted_iota(jnp.int32, shape, len(shape) - 1)


def norm(values, gain):
    mean_square = jnp.mean(values * values, axis=-1, keepdims=True)
    return values * lax.rsqrt(mean_square + 1e-06) * gain


def pack_factors(a_q, b_q, a_o, b_o, out, rows):
    start = pl.multiple_of((lax.axis_index("tp") % 2) * HALF, HALF)
    first = a_q[pl.ds(start, 80), :].astype(F32)
    second = a_q[pl.ds(start + 80, 80), :].astype(F32)
    rows[0:80, :] = jnp.concatenate([first, second], axis=1)
    bq = b_q[...].astype(F32)
    rows[BQ_AT : BQ_AT + 4, :] = bq[:, :HD]
    rows[BQ_AT + 4 : BQ_AT + 8, :] = bq[:, HD:]
    unit = lax.broadcasted_iota(jnp.int32, (256, 256), 0) == lanes((256, 256))
    ao = lax.dot_general(
        a_o[...], unit.astype(F32).astype(BF16), (((0,), (0,)), ((), ())), preferred_element_type=F32
    )
    rows[AO_AT : AO_AT + 4, :] = ao[:, :HD]
    rows[AO_AT + 4 : AO_AT + 8, :] = ao[:, HD:]
    bo = b_o[...].astype(F32)
    rows[BO_AT : BO_AT + 4, :] = bo[:, :HD]
    rows[BO_AT + 4 : BO_AT + 8, :] = bo[:, HD : 2 * HD]
    rows[BO_AT + 8 : BO_AT + 16, :] = jnp.zeros((8, HD), F32)
    rows[BO_AT + 8 : BO_AT + 12, 0:64] = bo[:, 2 * HD :]
    message = rows[...].astype(BF16)
    for g in range(GROUPS):
        out[g] = message


def low_rank(owner, tokens, factors, out, a_true):
    core = lax.axis_index("tp") % 2
    lane = lanes((80, HD))
    left = jnp.where(lane < R, 1.0, 0.0).astype(BF16)
    right = jnp.where(lane < R, 0.0, 1.0).astype(BF16)
    empty = jnp.zeros((HALF, HD), BF16)
    for g in range(GROUPS):
        base = owner[g] * BLOCK
        mine = pl.multiple_of(base + core * HALF, 32)
        other = pl.multiple_of(base + (1 - core) * HALF, 32)
        block = factors[g, 0:80, :]
        a_true[pl.ds(mine, 80), :] = block * left
        a_true[pl.ds(pl.multiple_of(mine + 80, 16), 80), :] = block * right
        a_true[pl.ds(other, HALF), :] = empty
    both = jnp.dot(tokens[...], a_true[...], preferred_element_type=F32)
    out[...] = both + pltpu.roll(both, R, 1)


def unpack_factors(factors, bq_out, ao_out, bo_out, rows):
    for at, pieces, out in ((BQ_AT, 2, bq_out), (AO_AT, 2, ao_out), (BO_AT, 3, bo_out)):
        for g in range(GROUPS):
            block = factors[g, BQ_AT:FACTOR_ROWS, :].astype(F32)
            for h in range(pieces):
                piece = block[at - BQ_AT + 4 * h : at - BQ_AT + 4 * h + 4]
                rows[4 * g : 4 * g + 4, HD * h : HD * h + HD] = piece
        whole = rows[:, : HD * pieces].astype(BF16)
        out[0:R, :] = whole
        out[R : 2 * R, :] = whole


def pack_queries(query_part, keyval_part, low_own, low_other, bq, q_gain, out, rows):
    low = low_own[...] + low_other[...]
    lane = lanes((ROWS, HD))
    high = low.astype(BF16).astype(F32)
    low_terms = jnp.where(lane < R, high, low - high).astype(BF16)
    query = query_part[...] + 0.5 * jnp.dot(low_terms, bq[...], preferred_element_type=F32)
    for e in range(2):
        normed = norm(query[:, HD * e : HD * e + HD], q_gain[...])
        for s in range(SEQS):
            at = PER_SEQ * s + STEPS * e
            rows[at : at + STEPS, :] = normed[STEPS * s : STEPS * s + STEPS]
    keyval = keyval_part[...]
    high = keyval.astype(BF16).astype(F32)
    rows[64:96, :] = jnp.concatenate([high, keyval - high], axis=1)
    message = rows[...].astype(BF16)
    for i in range(TP):
        out[i] = message


def cached_attention(lengths, received, cache, out, queries, weighted):
    first = lax.axis_index("tp") * SLOTS
    for i in range(TP):
        queries[i] = received[i, 0:64, :].astype(F32)
    position = lanes((ROWS, SLOTS)) + first
    lane = lanes((ROWS, HD))
    for c in range(KVH):
        logs = jnp.zeros((ROWS, HD), F32)
        for s in range(SEQS):
            rows = pl.ds(PER_SEQ * s, PER_SEQ)
            query = queries[4 * c : 4 * c + 4, rows, :].reshape(ROWS, HD).astype(BF16)
            scores = (
                lax.dot_general(query, cache[0, s, 0, c], NT, preferred_element_type=F32) * INV_ROOT
            )
            valid = position < lengths[0, s]
            scores = jnp.where(valid, scores, FAR)
            largest = scores.max(axis=-1, keepdims=True)
            weights = jnp.where(valid, jnp.exp(scores - largest), 0.0)
            total = weights.sum(axis=-1, keepdims=True)
            value = jnp.dot(weights.astype(BF16), cache[0, s, 1, c], preferred_element_type=F32)
            safe = jnp.where(total > 0.0, total, 1.0)
            value = value / safe
            log = jnp.where(total > 0.0, largest + jnp.log(safe), FAR)
            logs = jnp.where(lane % SEQS == s, log, logs)
            weighted[4 * c : 4 * c + 4, rows, :] = value.reshape(4, PER_SEQ, HD)
        high = logs.astype(BF16).astype(F32)
        middle = (logs - high).astype(BF16).astype(F32)
        terms = jnp.where(lane < 8, high, jnp.where(lane < 16, middle, logs - high - middle))
        weighted[4 * c : 4 * c + 4, 64:72, :] = terms.reshape(4, PER_SEQ, HD)
        weighted[4 * c : 4 * c + 4, 72:80, :] = jnp.zeros((4, 8, HD), F32)
    for i in range(TP):
        out[i] = weighted[i].astype(BF16)


def fresh_attention(received, k_gain, out, logs):
    me = lax.axis_index("tp")
    head = me // (TP // KVH)
    lane = lanes((ROWS, HD))

    def raw(left, right):
        pair = []
        for device in (left, right):
            terms = received[device, 64:96, :].astype(F32)
            pair.append(terms + pltpu.roll(terms, R, 1))
        return jnp.where(lane < R, pair[0], pair[1])

    keys = norm(raw(2 * head, 2 * head + 1), k_gain[...]).astype(BF16)
    values = raw(8 + 2 * head, 9 + 2 * head).astype(BF16)
    scores = (
        lax.dot_general(received[me, 0:64, :], keys, NT, preferred_element_type=F32) * INV_ROOT
    )
    row = lax.broadcasted_iota(jnp.int32, (64, ROWS), 0)
    column = lanes((64, ROWS))
    seen = (row // PER_SEQ == column // STEPS) & (row % STEPS >= column % STEPS)
    scores = jnp.where(seen, scores, FAR)
    largest = scores.max(axis=-1, keepdims=True)
    weights = jnp.where(seen, jnp.exp(scores - largest), 0.0)
    total = weights.sum(axis=-1, keepdims=True)
    value = jnp.dot(weights.astype(BF16), values, preferred_element_type=F32)
    out[...] = value / total
    log = largest + jnp.log(total)
    lane = lanes((PER_SEQ, HD))
    compact = jnp.zeros((PER_SEQ, HD), F32)
    for s in range(SEQS):
        compact = jnp.where(lane == s, log[PER_SEQ * s : PER_SEQ * s + PER_SEQ], compact)
    logs[...] = compact


def project(received, fresh, fresh_logs, ao, o_weight, out, attended):
    logs = []
    for i in range(TP):
        terms = received[i, 64:80, :].astype(F32)[0:8]
        logs.append(terms + pltpu.roll(terms, HD - 8, 1) + pltpu.roll(terms, HD - 16, 1))
    logs.append(fresh_logs[...])
    largest = functools.reduce(jnp.maximum, logs)
    shares = [jnp.exp(log - largest) for log in logs]
    inverse = 1.0 / functools.reduce(jnp.add, shares)
    shares = [share * inverse for share in shares]
    for pair in range(SEQS // 2):
        blocks = [received[i, 16 * pair : 16 * pair + 16, :].astype(F32) for i in range(TP)]
        for s in (2 * pair, 2 * pair + 1):
            at = PER_SEQ * s
            total = fresh[at : at + PER_SEQ, :] * shares[TP][:, s : s + 1]
            for i in range(TP):
                part = blocks[i][at - 16 * pair : at - 16 * pair + PER_SEQ]
                total = total + part * shares[i][:, s : s + 1]
            for e in range(2):
                attended[STEPS * s : STEPS * s + STEPS, HD * e : HD * e + HD] = total[
                    STEPS * e : STEPS * e + STEPS
                ]
    heads = attended[...].astype(BF16)
    low = lax.dot_general(heads, ao[...], NT, preferred_element_type=F32)
    lane = lanes((ROWS, HD))
    for k in range(TP // 2):
        at = 2 * OUT * k
        value = jnp.dot(heads, o_weight[:, at : at + 2 * OUT], preferred_element_type=F32)
        out[2 * k, :, 0 : 2 * HD] = value[:, 0 : 2 * HD].astype(BF16)
        middle = value[:, 2 * HD : 3 * HD]
        out[2 * k, :, 2 * HD : 3 * HD] = jnp.where(lane < R, middle, low).astype(BF16)
        out[2 * k + 1, :, 0:HD] = jnp.where(lane < R, low, middle).astype(BF16)
        out[2 * k + 1, :, HD : 3 * HD] = value[:, 3 * HD :].astype(BF16)


def finish(received, bo, out):
    odd = lax.axis_index("tp") % 2 == 1
    total = received[0].astype(F32)
    for i in range(1, TP):
        total = total + received[i].astype(F32)
    lane = lanes((ROWS, HD))
    low = jnp.where(
        odd,
        jnp.where(lane < R, total[:, :HD], 0.0),
        jnp.where(lane < R, 0.0, total[:, 2 * HD :]),
    )
    high = low.astype(BF16)
    rest = (low - high.astype(F32)).astype(BF16)
    extra = jnp.dot(high, bo[...], preferred_element_type=F32) + jnp.dot(
        rest, bo[...], preferred_element_type=F32
    )
    moved = pltpu.roll(total, 3 * HD - R, 1)
    result = (jnp.where(odd, moved, total) + 0.5 * extra)[:, :OUT].astype(BF16)
    for s in range(SEQS):
        out[0, s] = result[STEPS * s : STEPS * s + STEPS]


def call(kernel, in_specs, outs, scratch=(), cost=None):
    single = not isinstance(outs, (list, tuple))
    return pl.pallas_call(
        kernel,
        out_shape=outs,
        in_specs=in_specs,
        out_specs=VMEM if single else [VMEM] * len(outs),
        scratch_shapes=list(scratch),
        cost_estimate=pl.CostEstimate(
            flops=cost or 1_000_000, bytes_accessed=1_000_000, transcendentals=0
        ),
        compiler_params=pltpu.CompilerParams(vmem_limit_bytes=24 * 1024 * 1024),
    )


def shape(*dims, dtype=BF16):
    return jax.ShapeDtypeStruct(dims, dtype)


def per_device(
    hidden_in,
    q_weight,
    kv_weight,
    o_weight,
    q_gain,
    k_gain,
    cache,
    lengths,
    owner,
    a_q,
    b_q,
    a_o,
    b_o,
):
    tokens = hidden_in.reshape(ROWS, WIDTH)
    q_gain, k_gain = q_gain.reshape(1, HD), k_gain.reshape(1, HD)

    message = call(
        pack_factors,
        [VMEM] * 4,
        shape(GROUPS, FACTOR_ROWS, HD),
        [pltpu.VMEM((FACTOR_ROWS, HD), F32)],
    )(a_q, b_q, a_o, b_o)
    factors = lax.all_to_all(message, "group", 0, 0)

    query_part = jnp.dot(tokens, q_weight, preferred_element_type=F32)
    keyval_part = jnp.dot(tokens, kv_weight, preferred_element_type=F32)

    low_own = call(
        low_rank,
        [SMEM, VMEM, VMEM],
        shape(ROWS, HD, dtype=F32),
        [pltpu.VMEM((WIDTH, HD), BF16)],
    )(owner, tokens, factors)
    low_other = lax.ppermute(low_own, "tp", [(i, i ^ 1) for i in range(TP)])
    bq, ao, bo = call(
        unpack_factors,
        [VMEM],
        [shape(2 * R, 2 * HD), shape(2 * R, 2 * HD), shape(2 * R, 3 * HD)],
        [pltpu.VMEM((R, 3 * HD), F32)],
    )(factors)
    message = call(
        pack_queries,
        [VMEM] * 6,
        shape(TP, QKV_ROWS, HD),
        [pltpu.VMEM((QKV_ROWS, HD), F32)],
    )(query_part, keyval_part, low_own, low_other, bq, q_gain)
    received = lax.all_to_all(message, "tp", 0, 0)

    message = call(
        cached_attention,
        [SMEM, VMEM, VMEM],
        shape(TP, PART_ROWS, HD),
        [pltpu.VMEM((TP, 64, HD), F32), pltpu.VMEM((TP, PART_ROWS, HD), F32)],
    )(lengths, received, cache)
    parts = lax.all_to_all(message, "tp", 0, 0)
    fresh, fresh_logs = call(
        fresh_attention,
        [VMEM, VMEM],
        [shape(64, HD, dtype=F32), shape(PER_SEQ, HD, dtype=F32)],
    )(received, k_gain)

    message = call(
        project,
        [VMEM] * 5,
        shape(TP, ROWS, 3 * HD),
        [pltpu.VMEM((ROWS, 2 * HD), F32)],
    )(parts, fresh, fresh_logs, ao, o_weight)
    sums = lax.all_to_all(message, "tp", 0, 0)
    return call(finish, [VMEM, VMEM], shape(1, SEQS, STEPS, OUT))(sums, bo)


def solution(mesh):
    placed = (
        P("group", None, None, None),
        P(None, "tp"),
        P(None, "tp"),
        P("tp", None),
        P(),
        P(),
        P("group", None, None, None, "tp", None),
        P("group", None),
        P(),
        P("group", None),
        P("group", "tp"),
        P("tp", "group"),
        P("group", "tp"),
    )
    return jax.shard_map(
        per_device,
        mesh=mesh,
        in_specs=placed,
        out_specs=P("group", None, None, "tp"),
        check_vma=False,
    )
```

time: 380 us -> 89.3 us (0.23); the launches traced: 374 us -> 88.7 us
  blocking collectives: 286 us -> 24.9 us
  other arithmetic: 27.9 us -> 0 us
  waiting for transfers between devices: 0.05 us -> 21.6 us
  local copies, waits for them, and re-layouts: 28.5 us -> 8.26 us
  starting transfers between devices: 0.04 us -> 18.4 us
  matrix products: 17.4 us -> 1.92 us
  between operations: 13.7 us -> 0.1 us
  Pallas kernels: 0 us -> 13.5 us
    all_gather x8 -> x0, blocking collectives: 224 us -> none  [the longest x1 38 us: per_device(): lax.all_gather(b_q, 'group', axis=0, tiled=True)]
    psum x1 -> x0, blocking collectives: 62.8 us -> none  [per_device(): low_sum = lax.psum(low_part, 'tp')]
    all_to_all x0 -> x2, blocking collectives: none -> 24.9 us  [the longest x1 12.8 us: per_device(): received = lax.all_to_all(message, 'tp', 0, 0)]
    add x32 -> x0, other arithmetic: 24.3 us -> none  [the longest x15 23.1 us: join_parts(): earlier_part[2] * left_scale[..., None]]
    all_to_all x0 -> x2, waiting for transfers between devices: none -> 21.6 us  [the longest x1 14.4 us: per_device(): factors = lax.all_to_all(message, 'group', 0, 0)]
    all_to_all x0 -> x2, starting transfers between devices: none -> 16.1 us  [the longest x1 11.6 us: per_device(): factors = lax.all_to_all(message, 'group', 0, 0)]
    pallas_call x0 -> x8, Pallas kernels: none -> 13.5 us  [the longest x1 8.96 us: per_device(): call(cached_attention, [SMEM, VMEM, VMEM], shape(TP, PART_ROWS, HD), [plt...]
    dot_general x11 -> x2, matrix products: 14.7 us -> 1.92 us  [the longest x1 1.37 us: per_device(): keyval_part = jnp.dot(tokens, kv_weight, preferred_element_type=F32)]
  transfers between devices with their start and end apart: 2 -> 3, of which waited for: 0 -> 2; matrix products, arithmetic and copies ran while one was open for 4% -> 3% of each run, Pallas kernels for 0% -> 1%
where the time goes in v1:
time: 89.3 us; the launch traced here: 88.7 us
  blocking collectives  24.9 us (28%)
  waiting for transfers between devices  21.6 us (24%)
  starting transfers between devices  18.4 us (21%)
  Pallas kernels  13.5 us (15%)
  local copies, waits for them, and re-layouts  8.26 us (9%)
  matrix products  1.92 us (2%)
    all_to_all x1, waiting for transfers between devices, per_device(): factors = lax.all_to_all(message, 'group', 0, 0)  14.4 us
    all_to_all x1, blocking collectives, per_device(): received = lax.all_to_all(message, 'tp', 0, 0)  12.8 us
    all_to_all x1, blocking collectives, per_device(): sums = lax.all_to_all(message, 'tp', 0, 0)  12.1 us
    all_to_all x1, starting transfers between devices, per_device(): factors = lax.all_to_all(message, 'group', 0, 0)  11.6 us
    pallas_call x1, Pallas kernels, per_device(): call(cached_attention, [SMEM, VMEM, VMEM], shape(TP, PART_ROWS, HD), [plt...  8.96 us
    all_to_all x1, waiting for transfers between devices, per_device(): parts = lax.all_to_all(message, 'tp', 0, 0)  7.25 us
    unnamed x20, local copies, waits for them, and re-layouts  7.21 us
    all_to_all x1, starting transfers between devices, per_device(): parts = lax.all_to_all(message, 'tp', 0, 0)  4.5 us
  transfers between devices with their start and end apart: 3, of which 2 were waited for; matrix products, arithmetic and copies ran while one was open for 3% of the time, Pallas kernels for 1%

profile of v1, /device:TPU:1, one launch (start us, length us, event | category | flops | bytes accessed | tf_op | source)
XLA Modules:
  0.0 88.7 jit_solution(9627063209075606063)
XLA Ops:
  0.0 0.0 copy-start
  0.0 1.0 %copy.15.a_o = bf16[256,4]{1,0:T(8,128)(2,1)S(1)} copy(bf16[256,4]{0,1:T(4,128)(2,1)} %param.24) | data formatting | bytes 4096 | tf_op args[11]
  1.0 0.9 %copy.14.a_q = bf16[320,64]{1,0:T(8,128)(2,1)S(1)} copy(bf16[320,64]{0,1:T(8,128)(2,1)} %param.22) | data formatting | bytes 81920 | tf_op args[9]
  1.9 0.0 copy-start.3
  1.9 0.7 copy-done.3
  2.6 0.7 copy-done.4
  3.3 0.9 %shard_map.127 = bf16[16,112,128]{2,1,0:T(8,128)(2,1)} custom-call(bf16[320,64]{1,0:T(8,128)(2,1)S(1)} %copy.14.a_q, bf16[4,256]{1,0:T(4,128)(2,1)S(1)} %copy-done.4, bf16[256,4]{1,0:T(8,128)(2,1)S(1)} %copy.15.a_o, bf16[4,320]{1,0:T(4,128)(2,1)S(1)} %copy-done.3), custom_call_target="tpu_custom_call" | custom-call | flops 1000000 | bytes 1000000 | tf_op jit(solution)/shard_map/pallas_call | solution.py:287
  4.2 11.6 %all-to-all-start = ((bf16[16,112,128]{2,1,0:T(8,128)(2,1)}), bf16[16,112,128]{2,1,0:T(8,128)(2,1)S(1)}, u32[]{:S(2)}, u32[]{:S(2)}) async-start(bf16[16,112,128]{2,1,0:T(8,128)(2,1)} %shard_map.127), calls=%async_computation | async-start | bytes 917504 | tf_op jit(solution)/shard_map/all_to_all | solution.py:293
  15.8 1.1 %reshape.9.tokens = bf16[32,5120]{1,0:T(8,128)(2,1)S(1)} reshape(bf16[1,8,4,5120]{3,2,1,0:T(4,128)(2,1)} %param.13) | data formatting | bytes 655360 | tf_op jit(solution)/shard_map/reshape | solution.py:284
  16.9 0.0 copy-done
  16.9 0.0 copy-start.5
  16.9 0.0 copy-start.6
  16.9 0.5 fusion.query_part
  17.4 14.4 %all-to-all-done.factors = bf16[16,112,128]{2,1,0:T(8,128)(2,1)S(1)} async-done(((bf16[16,112,128]{2,1,0:T(8,128)(2,1)}), bf16[16,112,128]{2,1,0:T(8,128)(2,1)S(1)}, u32[]{:S(2)}, u32[]{:S(2)}) %all-to-all-start) | async-done | bytes 458784 | tf_op jit(solution)/shard_map/all_to_all | solution.py:293
  31.8 0.0 copy-done.8
  31.8 1.1 %shard_map.128.low_own = f32[32,128]{1,0:T(8,128)S(1)} custom-call(s32[16]{0:T(128)S(1)} %copy-done.8, bf16[32,5120]{1,0:T(8,128)(2,1)S(1)} %reshape.9.tokens, bf16[16,112,128]{2,1,0:T(8,128)(2,1)S(1)} %all-to-all-done.factors), custom_call_target="tpu_custom_call" | custom-call | flops 1000000 | bytes 1000000 | tf_op jit(solution)/shard_map/pallas_call | solution.py:298
  32.9 2.3 %collective-permute-start = (f32[32,128]{1,0:T(8,128)S(1)}, f32[32,128]{1,0:T(8,128)S(1)}, u32[]{:S(2)}, u32[]{:S(2)}) collective-permute-start(f32[32,128]{1,0:T(8,128)S(1)} %shard_map.128.low_own), channel_id=1, source_target_pairs={{0,1},{1,0},{2,3},{3,2},{4,5},{5,4},{6,7},{7,6},{8,9},{9,8},{10,11... | collective-permute-start | bytes 49160 | tf_op jit(solution)/shard_map/ppermute | solution.py:304
  35.2 1.4 %fusion.1.keyval_part = f32[32,64]{1,0:T(8,128)S(1)} fusion(bf16[32,5120]{1,0:T(8,128)(2,1)S(1)} %reshape.9.tokens, bf16[5120,64]{0,1:T(8,128)(2,1)} %param.15), kind=kOutput, calls=%fused_computation.1 | convolution fusion | flops 20971520 | bytes 991232 | tf_op jit(solution)/shard_map/dot_general | solution.py:296
  36.6 0.1 shard_map.129
  36.7 0.0 collective-permute-done.low_other
  36.7 0.0 copy-done.5
  36.7 0.3 shard_map.130
  37.0 12.8 %all_to_all.20.received = bf16[16,96,128]{2,1,0:T(8,128)(2,1)S(1)} all-to-all(bf16[16,96,128]{2,1,0:T(8,128)(2,1)S(1)} %shard_map.130), channel_id=1, replica_groups=mesh['group'=16,'tp'=16] {'tp'}, dimensions={0} | all-to-all | bytes 786432 | tf_op jit(solution)/shard_map/all_to_all | solution.py:317
  49.8 2.2 %copy-done.1 = bf16[1,8,2,4,256,128]{5,4,3,2,1,0:T(8,128)(2,1)S(1)} copy-done((bf16[1,8,2,4,256,128]{5,4,3,2,1,0:T(8,128)(2,1)S(1)}, bf16[1,8,2,4,256,128]{5,4,3,2,1,0:T(8,128)(2,1)}, u32[]{:S(2)}) %copy-start.1) | copy-done | bytes 4194328
  52.0 9.0 %shard_map.131 = bf16[16,80,128]{2,1,0:T(8,128)(2,1)} custom-call(s32[1,8]{1,0:T(1,128)S(1)} %copy-done.6, bf16[16,96,128]{2,1,0:T(8,128)(2,1)S(1)} %all_to_all.20.received, bf16[1,8,2,4,256,128]{5,4,3,2,1,0:T(8,128)(2,1)S(1)} %copy-done.1), custom_call_target="tpu_custom_call" | custom-call | flops 1000000 | bytes 1000000 | tf_op jit(solution)/shard_map/pallas_call | solution.py:319
  60.9 4.5 %all-to-all-start.2 = ((bf16[16,80,128]{2,1,0:T(8,128)(2,1)}), bf16[16,80,128]{2,1,0:T(8,128)(2,1)S(1)}, u32[]{:S(2)}, u32[]{:S(2)}) async-start(bf16[16,80,128]{2,1,0:T(8,128)(2,1)} %shard_map.131), calls=%async_computation.2 | async-start | bytes 655360 | tf_op jit(solution)/shard_map/all_to_all | solution.py:325
  65.4 0.5 shard_map.132
  65.9 7.3 %all-to-all-done.2.received = bf16[16,80,128]{2,1,0:T(8,128)(2,1)S(1)} async-done(((bf16[16,80,128]{2,1,0:T(8,128)(2,1)}), bf16[16,80,128]{2,1,0:T(8,128)(2,1)S(1)}, u32[]{:S(2)}, u32[]{:S(2)}) %all-to-all-start.2) | async-done | bytes 327712 | tf_op jit(solution)/shard_map/all_to_all | solution.py:325
  73.2 1.7 %copy-done.2 = bf16[256,5120]{1,0:T(8,128)(2,1)S(1)} copy-done((bf16[256,5120]{1,0:T(8,128)(2,1)S(1)}, bf16[256,5120]{1,0:T(8,128)(2,1)}, u32[]{:S(2)}) %copy-start.2) | copy-done | bytes 2621464
  74.9 0.9 %shard_map.133 = bf16[16,32,384]{2,1,0:T(8,128)(2,1)S(1)} custom-call(bf16[16,80,128]{2,1,0:T(8,128)(2,1)S(1)} %all-to-all-done.2.received, f32[64,128]{1,0:T(8,128)S(1)} %get-tuple-element.11.fresh, f32[8,128]{1,0:T(8,128)S(1)} %get-tuple-element.12.fresh_logs, bf16[128,256]{1,0:T(8,128)(2,1)S(1)} %get-tuple-element.13.ao, bf16[256,5120]{1,0:T(8,128)(2,1)S(1)} %copy-done.2), custom_call_target="tpu_custom_call" | custom-call | flops 1000000 | bytes 1000000 | tf_op jit(solution)/shard_map/pallas_call | solution.py:332
  75.9 12.1 %all_to_all.21.received = bf16[16,32,384]{2,1,0:T(8,128)(2,1)S(1)} all-to-all(bf16[16,32,384]{2,1,0:T(8,128)(2,1)S(1)} %shard_map.133), channel_id=1, replica_groups=mesh['group'=16,'tp'=16] {'tp'}, dimensions={0} | all-to-all | bytes 786432 | tf_op jit(solution)/shard_map/all_to_all | solution.py:338
  87.9 0.8 shard_map.134
  (7 shorter events, 0.0 us)
Async XLA Ops:
  0.0 16.9 %copy-start = (bf16[5120,256]{1,0:T(8,128)(2,1)S(1)}, bf16[5120,256]{1,0:T(8,128)(2,1)}, u32[]{:S(2)}) copy-start(bf16[5120,256]{1,0:T(8,128)(2,1)} %param.14) | copy-start | bytes 7864324
  1.0 30.9 %copy-start.8 = (s32[16]{0:T(128)S(1)}, s32[16]{0:T(128)}, u32[]{:S(2)}) copy-start(s32[16]{0:T(128)} %owner.1) | copy-start | bytes 196
  1.9 0.7 copy-start.3
  2.6 0.7 copy-start.4
  4.2 27.6 %all-to-all-start = ((bf16[16,112,128]{2,1,0:T(8,128)(2,1)}), bf16[16,112,128]{2,1,0:T(8,128)(2,1)S(1)}, u32[]{:S(2)}, u32[]{:S(2)}) async-start(bf16[16,112,128]{2,1,0:T(8,128)(2,1)} %shard_map.127), calls=%async_computation | async-start | bytes 917504 | tf_op jit(solution)/shard_map/all_to_all | solution.py:293
  16.9 19.8 %copy-start.5 = (f32[128]{0:T(128)S(1)}, f32[128]{0:T(128)}, u32[]{:S(2)}) copy-start(f32[128]{0:T(128)} %param.17) | copy-start | bytes 1540
  16.9 32.9 %copy-start.6 = (s32[1,8]{1,0:T(1,128)S(1)}, s32[1,8]{1,0:T(1,128)}, u32[]{:S(2)}) copy-start(s32[1,8]{1,0:T(1,128)} %lengths.1) | copy-start | bytes 100
  32.9 3.8 %collective-permute-start = (f32[32,128]{1,0:T(8,128)S(1)}, f32[32,128]{1,0:T(8,128)S(1)}, u32[]{:S(2)}, u32[]{:S(2)}) collective-permute-start(f32[32,128]{1,0:T(8,128)S(1)} %shard_map.128.low_own), channel_id=1, source_target_pairs={{0,1},{1,0},{2,3},{3,2},{4,5},{5,4},{6,7},{7,6},{8,9},{9,8},{10,11... | collective-permute-start | bytes 49160 | tf_op jit(solution)/shard_map/ppermute | solution.py:304
  49.8 2.2 %copy-start.1 = (bf16[1,8,2,4,256,128]{5,4,3,2,1,0:T(8,128)(2,1)S(1)}, bf16[1,8,2,4,256,128]{5,4,3,2,1,0:T(8,128)(2,1)}, u32[]{:S(2)}) copy-start(bf16[1,8,2,4,256,128]{5,4,3,2,1,0:T(8,128)(2,1)} %cache.1) | copy-start | bytes 12582916
  52.0 13.5 %copy-start.7 = (f32[128]{0:T(128)S(1)}, f32[128]{0:T(128)}, u32[]{:S(2)}) copy-start(f32[128]{0:T(128)} %param.18) | copy-start | bytes 1540
  60.9 12.3 %all-to-all-start.2 = ((bf16[16,80,128]{2,1,0:T(8,128)(2,1)}), bf16[16,80,128]{2,1,0:T(8,128)(2,1)S(1)}, u32[]{:S(2)}, u32[]{:S(2)}) async-start(bf16[16,80,128]{2,1,0:T(8,128)(2,1)} %shard_map.131), calls=%async_computation.2 | async-start | bytes 655360 | tf_op jit(solution)/shard_map/all_to_all | solution.py:325
  73.2 1.7 %copy-start.2 = (bf16[256,5120]{1,0:T(8,128)(2,1)S(1)}, bf16[256,5120]{1,0:T(8,128)(2,1)}, u32[]{:S(2)}) copy-start(bf16[256,5120]{1,0:T(8,128)(2,1)} %o_weight.1) | copy-start | bytes 7864324
